TPU v7x, 256 devices: a whole 4x4x8 slice. The times are simulated.
256 devices in a mesh: dp: 16 (over y, x_hi, core), mp: 16 (over z, x_lo).
Axes of the slice: x: 4 (x_hi: 2, x_lo: 2; x = x_hi * 2 + x_lo), y: 4, z: 8, core: 2. Of those that a mesh axis runs over, the one named last changes fastest.
Arguments:
- tokens: bfloat16 [8192, 6144], P('dp', 'mp'), may hold values from -6 to 6
- ln_gain: float32 [6144], replicated, may hold values from 0.1 to 1.9
- projected: bfloat16 [8192, 3, 4096], P('dp', None, 'mp'), may hold values from -12.5 to 12.5, as said below
- out_grad: bfloat16 [8192, 4096], P('dp', 'mp'), may hold values from -24 to 24
- w_joined: bfloat16 [6144, 3, 4096], P(None, None, 'mp'), may hold values from -0.078125 to 0.078125
Outputs:
- grad_weight: float32 [6144, 3, 4096], P('dp', None, 'mp')
- grad_input: bfloat16 [8192, 6144], P('dp', 'mp')
Inputs may be any that keep to these rules, and one draw needn't show every extreme that they name: `projected`: each token's query, key and value projections, heads in order.
All inputs are finite; a program needn't handle non-finite values.
Results may differ from a plain program's by a relative error of at most 0.017.
Values may be sent and summed in bfloat16 or wider, within the bound.
A program may use at most 192 MiB of HBM per device.

v0:
```python
import jax
import jax.numpy as jnp
from jax import lax
from jax.sharding import PartitionSpec as P

D = 6144
HDIM = 128
SEQ = 512


def product(form, left, right):
    return jnp.einsum(form, left, right, preferred_element_type=jnp.float32)


def attention_grad(projected, out_grad):
    queries = projected[:, :, 0]
    keys_all = projected[:, :, 1]
    values = projected[:, :, 2]
    scaling = projected.shape[-1] ** (-0.5)
    scores = product("bqhd,bkhd->bhqk", queries, keys_all) * scaling
    raised = jnp.exp(scores - jnp.max(scores, axis=-1, keepdims=True))
    attn_probs = raised / jnp.sum(raised, axis=-1, keepdims=True)
    probs_low = attn_probs.astype(jnp.bfloat16)
    value_grad = product("bhqk,bqhd->bkhd", probs_low, out_grad)
    prob_grad = product("bqhd,bkhd->bhqk", out_grad, values)
    score_grad = attn_probs * (prob_grad - jnp.sum(attn_probs * prob_grad, axis=-1, keepdims=True))
    score_low = score_grad.astype(jnp.bfloat16)
    query_grad = product("bhqk,bkhd->bqhd", score_low, keys_all) * scaling
    key_grad = product("bhqk,bqhd->bkhd", score_low, queries) * scaling
    return jnp.stack([query_grad, key_grad, value_grad], axis=2).astype(jnp.bfloat16)


def normalize(tokens):
    values = tokens.astype(jnp.float32)
    center = jnp.mean(values, axis=-1, keepdims=True)
    spread = jnp.mean(jnp.square(values - center), axis=-1, keepdims=True)
    inverse = lax.rsqrt(spread + 1e-06)
    return ((values - center) * inverse, inverse)


def shards(tokens, ln_gain, projected, out_grad, w_joined):
    gathered = lax.all_gather(tokens, "mp", axis=1, tiled=True)
    x_hat, inverse = normalize(gathered)
    normed = (x_hat * ln_gain).astype(jnp.bfloat16)
    row_count = projected.shape[0]
    width = projected.shape[2]
    local_heads = width // HDIM
    images = row_count // SEQ
    grad_proj = attention_grad(
        projected.reshape(images, SEQ, 3, local_heads, HDIM),
        out_grad.reshape(images, SEQ, local_heads, HDIM),
    )
    grad_flat = grad_proj.reshape(row_count, 3 * width)
    w_flat = w_joined.reshape(D, 3 * width)
    weight_rows = D // lax.axis_size("dp")
    sliced = normed
    grad_weight = lax.psum_scatter(
        lax.dot_general(
            sliced, grad_flat, (((0,), (0,)), ((), ())), preferred_element_type=jnp.float32
        ).astype(jnp.bfloat16),
        "dp",
        scatter_dimension=0,
        tiled=True,
    ).astype(jnp.float32)
    share = D // lax.axis_size("mp")
    sliced = w_flat
    grad_share = lax.psum_scatter(
        lax.dot_general(
            sliced, grad_flat, (((1,), (1,)), ((), ())), preferred_element_type=jnp.float32
        ),
        "mp",
        scatter_dimension=0,
        tiled=True,
    ).T
    first_col = lax.axis_index("mp") * share
    gain_share = lax.dynamic_slice_in_dim(ln_gain, first_col, share, 0)
    hat_share = lax.dynamic_slice_in_dim(x_hat, first_col, share, 1)
    scaled = grad_share * gain_share
    sum_plain, sum_hat = lax.psum(
        (jnp.sum(scaled, axis=-1), jnp.sum(scaled * hat_share, axis=-1)), "mp"
    )
    mean_plain = sum_plain[:, None] / D
    mean_hat = sum_hat[:, None] / D
    grad_input = ((scaled - mean_plain - hat_share * mean_hat) * inverse).astype(jnp.bfloat16)
    return (grad_weight.reshape(weight_rows, 3, width), grad_input)


def solution(mesh):
    in_specs = (P("dp", "mp"), P(), P("dp", None, "mp"), P("dp", "mp"), P(None, None, "mp"))
    out_specs = (P("dp", None, "mp"), P("dp", "mp"))
    return jax.shard_map(shards, mesh=mesh, in_specs=in_specs, out_specs=out_specs, check_vma=False)
```

profile of v0, /device:TPU:1, one launch (start us, length us, event | category | flops | bytes accessed | tf_op | source)
XLA Modules:
  0.0 553.4 jit_solution(1299797854848527579)
XLA Ops:
  7.2 0.7 all-gather.2.cloned.1.call-update
  7.9 1.4 copy.15
  9.4 1.1 copy.37
  10.5 12.7 %copy.27 = bf16[6144,3,256]{0,2,1:T(8,128)(2,1)} copy(bf16[6144,3,256]{2,0,1:T(8,128)(2,1)} %param.9) | data formatting | bytes 18874368 | tf_op args[4]
  23.1 0.9 fusion.18
  24.1 0.5 multiply_reduce_fusion
  24.6 0.5 multiply_convert_fusion.2
  25.9 0.5 convolution_bitcast_fusion.1
  26.5 1.2 slice-done.1
  28.1 8.3 %convolution_bitcast_fusion = f32[6144,512]{0,1:T(8,128)} fusion(bf16[512,768]{0,1:T(8,128)(2,1)S(1)} %bitcast.86, bf16[6144,768]{0,1:T(8,128)(2,1)S(1)} %bitcast.85), kind=kOutput, calls=%fused_computation.8 | convolution fusion | flops 4831838208 | bytes 22806528 | tf_op jit(solution)/shard_map/dot_general | solution.py:68
  36.6 117.4 %all-gather.2.cloned.1.call-done = bf16[512,6144]{1,0:T(8,128)(2,1)} async-done(((bf16[512,384]{1,0:T(8,128)(2,1)}), bf16[512,6144]{1,0:T(8,128)(2,1)}) %all-gather.2.cloned.1.call-update) | async-done | bytes 6291472 | tf_op jit(solution)/shard_map/all_gather | solution.py:42
  154.0 3.8 convert_reduce_fusion
  157.8 0.7 copy-done
  158.6 1.8 fusion.3
  160.4 8.7 %convolution_convert_fusion = bf16[6144,768]{1,0:T(8,128)(2,1)} fusion(bf16[512,768]{0,1:T(8,128)(2,1)S(1)} %bitcast.87, f32[6144]{0:T(1024)S(1)} %copy-done.1, bf16[512,6144]{1,0:T(8,128)(2,1)S(1)} %copy-done, f32[512]{0:T(512)S(1)} %add_rsqrt_fusion, f32[512]{0:T(512)S(1)} %broadcast_multiply_fusion.2), kind=kOutput, calls=%fused_computation.7 | convolution fusion | flops 4852285440 | bytes 16543744 | tf_op jit(solution)/shard_map/dot_general | solution.py:58
  169.2 9.8 %fusion.1 = f32[512,6144]{1,0:T(8,128)} fusion(bf16[512,6144]{1,0:T(8,128)(2,1)} %all-gather.2.cloned.1.call-done, f32[512]{0:T(512)S(1)} %add_rsqrt_fusion, f32[512]{0:T(512)S(1)} %broadcast_multiply_fusion.2), kind=kLoop, calls=%fused_computation.3 | loop fusion | flops 9437184 | bytes 18878464 | tf_op jit(solution)/shard_map/mul | solution.py:38
  179.0 246.0 %reduce-scatter.5.cloned.1.call-done = f32[384,512]{0,1:T(8,128)} async-done(((f32[6144,512]{0,1:T(8,128)}), f32[384,512]{0,1:T(8,128)}) %reduce-scatter.5.cloned.1.call-update) | async-done | bytes 786448 | tf_op jit(solution)/shard_map/reduce_scatter | solution.py:67
  425.0 1.3 multiply_reduce_fusion.2
  426.3 1.5 fusion.13
  427.9 26.0 %all-reduce = (f32[512]{0:T(512)S(1)}, f32[512]{0:T(512)S(1)}) all-reduce(f32[512]{0:T(512)S(1)} %fusion.13, f32[512]{0:T(512)S(1)} %multiply_reduce_fusion.2), channel_id=1, replica_groups=mesh['dp'=16,'mp'=16] {'mp'}, use_global_device_ids=true, to_apply=%region_10.0 | all-reduce | flops 1024 | bytes 8192 | tf_op jit(solution)/shard_map/psum | solution.py:79
  453.9 2.6 fusion.12
  456.5 87.7 %reduce-scatter.3.cloned.1.call-done = bf16[384,768]{1,0:T(8,128)(2,1)} async-done(((bf16[6144,768]{1,0:T(8,128)(2,1)}), bf16[384,768]{1,0:T(8,128)(2,1)}) %reduce-scatter.3.cloned.1.call-update) | async-done | bytes 589840 | tf_op jit(solution)/shard_map/reduce_scatter | solution.py:57
  544.2 1.3 copy.26
  545.5 1.4 copy.28
  (21 shorter events, 1.6 us)
Async XLA Ops:
  7.2 146.8 %all-gather.2.cloned.1.call-start = ((), (), s32[]{:S(2)}) async-start(), calls=%async_computation.2 | async-start | bytes 6684672 | tf_op jit(solution)/shard_map/all_gather | solution.py:42
  7.9 417.1 %reduce-scatter.5.cloned.1.call-start = ((), (), s32[]{:S(2)}) async-start(), calls=%async_computation.4 | async-start | bytes 13369344 | tf_op jit(solution)/shard_map/reduce_scatter | solution.py:67
  24.1 2.5 slice-start
  24.6 3.2 slice-start.1
  25.9 2.1 slice-start.2
  36.4 124.0 %copy-start.1 = (f32[6144]{0:T(1024)S(1)}, f32[6144]{0:T(1024)}, u32[]{:S(2)}) copy-start(f32[6144]{0:T(1024)} %param.6) | copy-start | bytes 73732
  36.4 507.8 %reduce-scatter.3.cloned.1.call-start = ((), (), s32[]{:S(2)}) async-start(), calls=%async_computation.3 | async-start | bytes 10027008 | tf_op jit(solution)/shard_map/reduce_scatter | solution.py:57
  154.0 4.6 copy-start
Sparse Core Ops, SparseCore 0:
  9.8 144.1 all-gather.1
  156.5 268.4 reduce-scatter.4
  429.7 114.4 reduce-scatter.2
where the time goes:
time: 554 us; the launch traced here: 553 us
  waiting for transfers between devices  452 us (82%)
  blocking collectives  26 us (5%)
  other arithmetic  21.5 us (4%)
  local copies, waits for them, and re-layouts  20.2 us (4%)
  matrix products  19.7 us (4%)
  between operations  13.8 us (2%)
    reduce_scatter x1, waiting for transfers between devices, shards(): lax.psum_scatter(lax.dot_general(sliced, grad_flat, (((1,), (1,)), ((), (...  246 us
    all_gather x1, waiting for transfers between devices, shards(): gathered = lax.all_gather(tokens, 'mp', axis=1, tiled=True)  117 us
    reduce_scatter x1, waiting for transfers between devices, shards(): lax.psum_scatter(lax.dot_general(sliced, grad_flat, (((0,), (0,)), ((), (...  87.7 us
    psum x1, blocking collectives, shards(): lax.psum((jnp.sum(scaled, axis=-1), jnp.sum(scaled * hat_share, axis=-1))...  26 us
    unnamed x13, local copies, waits for them, and re-layouts  17.8 us
  transfers between devices with their start and end apart: 3, of which 3 were waited for; matrix products, arithmetic and copies ran while one was open for 10% of the time, Pallas kernels for 0%

commit v1 on v0

v1 whole, which is shorter than its diff:
```python
import functools

import jax
import jax.numpy as jnp
from jax import lax
from jax.experimental import pallas as pl
from jax.experimental.pallas import tpu as pltpu
from jax.sharding import PartitionSpec as P

MESH = pl.DeviceIdType.MESH
F32 = jnp.float32
BF16 = jnp.bfloat16

D = 6144
HDIM = 128
SEQ = 512
COLS = 384
WIDTH = 256
HALF = SEQ // 2
GROWS = 3 * WIDTH
GHALF = GROWS // 2
SCALE = HDIM ** (-0.5)
LANES = 128

NT = (((1,), (1,)), ((), ()))
NN = (((1,), (0,)), ((), ()))
TN = (((0,), (0,)), ((), ()))


def slot(dz, dx):
    m = 7 if abs(dz) == 4 else (2 * abs(dz) - (1 if dz < 0 else 0))
    return dx * 8 + m


GATHER = [
    ("z+", (0, 0), None), ("z-", (0, 0), None), ("x", (0, 0), None),
    ("z+", (-1, 0), None), ("z-", (1, 0), None), ("x", (-1, 0), None),
    ("z+", (-2, 0), None), ("z-", (2, 0), None), ("x", (-2, 0), None),
    ("z+", (-3, 0), 0), ("z-", (3, 0), 1), ("x", (2, 0), None),
    ("z+", (-2, 1), None), ("x", (1, 0), None),
    ("z-", (2, 1), None), ("z+", (-3, 1), 0), ("z-", (3, 1), 1),
]


def dot(left, right, dims):
    return lax.dot_general(left, right, dims, preferred_element_type=F32)


def add_into(dst, sources, rows, chunk=64):
    def body(i, carry):
        at = pl.ds(pl.multiple_of(i * chunk, chunk), chunk)
        total = dst[at, :].astype(F32)
        for source in sources:
            total = total + source[at, :].astype(F32)
        dst[at, :] = total.astype(BF16)
        return carry

    lax.fori_loop(0, rows // chunk, body, 0)


def pack_rows(acc, out, first):
    for i in range(4):
        part = acc[i * LANES : (i + 1) * LANES, :]
        out[first + i : first + i + 1, :] = jnp.sum(part.T, axis=0, keepdims=True)


def spread_rows(rows, out):
    for i in range(4):
        out[i * LANES : (i + 1) * LANES, :] = jnp.broadcast_to(rows[i : i + 1, :], (LANES, LANES)).T


def kernel(
    tok, gain, proj, og, w, gw_out, gi_out,
    ag, wv, pv, ov, gp, gpt, part, halves, landed, gsum, cland, yland, yhalf, xland, normed,
    acc_a, acc_b, mean_b, inv_b, st_send, st_recv, sz_send, sz_recv,
    load_sem, ag_s, ag_r, st_s, st_r, sz_s, sz_r, rs_s, rs_r, c_s, c_r, y_s, y_r,
):
    dp, mp = lax.axis_index("dp"), lax.axis_index("mp")
    y, xh, c = dp // 4, (dp // 2) % 2, dp % 2
    z, x = mp // 2, mp % 2

    def at_z(k):
        return (dp, ((z + k + 8) % 8) * 2 + x)

    at_x = (dp, z * 2 + 1 - x)
    at_c = (y * 4 + xh * 2 + 1 - c, mp)
    at_xh = (y * 4 + (1 - xh) * 2 + c, mp)

    def at_y(k):
        return (((y + k + 4) % 4) * 4 + xh * 2 + c, mp)

    def remote(src, dst, send, recv, device):
        return pltpu.make_async_remote_copy(
            src_ref=src, dst_ref=dst, send_sem=send, recv_sem=recv, device_id=device, device_id_type=MESH
        )

    loads = [
        pltpu.make_async_copy(tok, ag.at[0], load_sem.at[0]),
        pltpu.make_async_copy(proj, pv, load_sem.at[1]),
        pltpu.make_async_copy(og, ov, load_sem.at[2]),
        pltpu.make_async_copy(w, wv, load_sem.at[3]),
    ]
    for load in loads:
        load.start()

    barrier = pltpu.get_barrier_semaphore()
    peers = [at_z(k) for k in range(1, 8)] + [at_x, at_c, at_xh, at_y(1), at_y(-1)]
    for peer in peers:
        pl.semaphore_signal(barrier, inc=1, device_id=peer, device_id_type=MESH)
    pl.semaphore_wait(barrier, len(peers))

    def gather(e):
        channel, (dz, dx), half = GATHER[e]
        if channel == "x":
            there, device = slot(dz, 1 - dx), at_x
        else:
            step = 1 if channel == "z+" else -1
            there, device = slot(dz - step, dx), at_z(step)
        here = slot(dz, dx)
        if half is None:
            src = tok if here == 0 else ag.at[here]
            dst = ag.at[there]
        else:
            src = ag.at[here, pl.ds(half * HALF, HALF)]
            dst = ag.at[there, pl.ds(half * HALF, HALF)]
        return remote(src, dst, ag_s.at[e], ag_r.at[e], device)

    for e in (0, 1, 2):
        gather(e).start()

    def exchange_x(n):
        return remote(st_send.at[n], st_recv.at[n], st_s.at[n], st_r.at[n], at_x)

    def exchange_z(n, k):
        return remote(sz_send.at[n], sz_recv.at[n, k], sz_s.at[n, k], sz_r.at[n, k], at_z(k))

    loads[0].wait()
    for i in range(4):
        rows = slice(i * LANES, (i + 1) * LANES)
        tiles = [ag[0, rows, k * LANES : (k + 1) * LANES].astype(F32) for k in range(3)]
        sums = tiles[0] + tiles[1] + tiles[2]
        center = jnp.sum(sums, axis=1, keepdims=True) / COLS
        acc_a[rows, :] = sums
        acc_b[rows, :] = sum(jnp.square(tile - center) for tile in tiles)
    pack_rows(acc_a, st_send.at[0], 0)
    pack_rows(acc_b, st_send.at[0], 4)
    st_send[0, 0:4, :] = st_send[0, 0:4, :] / COLS
    exchange_x(0).start()

    def head(h):
        cols = slice(h * HDIM, (h + 1) * HDIM)
        queries, keys_all, values, upstream = pv[0, :, cols], pv[1, :, cols], pv[2, :, cols], ov[:, cols]
        key_grad = value_grad = None
        for q0 in range(0, SEQ, 256):
            qs = slice(q0, q0 + 256)
            scores = dot(keys_all, queries[qs], NT) * SCALE
            raised = jnp.exp(scores - jnp.max(scores, axis=0, keepdims=True))
            probs = raised / jnp.sum(raised, axis=0, keepdims=True)
            term = dot(probs.astype(BF16), upstream[qs], NN)
            value_grad = term if value_grad is None else value_grad + term
            prob_grad = dot(values, upstream[qs], NT)
            score_grad = probs * (prob_grad - jnp.sum(probs * prob_grad, axis=0, keepdims=True))
            score_low = score_grad.astype(BF16)
            term = dot(score_low, queries[qs], NN)
            key_grad = term if key_grad is None else key_grad + term
            gp[0, qs, cols] = (dot(score_low, keys_all, TN) * SCALE).astype(BF16)
        gp[1, :, cols] = (key_grad * SCALE).astype(BF16)
        gp[2, :, cols] = value_grad.astype(BF16)

    loads[1].wait()
    loads[2].wait()
    head(0)

    exchange_x(0).wait_recv()
    mine, other = st_send[0], st_recv[0]
    center = (mine[0:4] + other[0:4]) * 0.5
    sz_send[0, 0:4, :] = center
    sz_send[0, 4:8, :] = mine[4:8] + other[4:8] + COLS * (
        jnp.square(mine[0:4] - center) + jnp.square(other[0:4] - center)
    )
    for k in range(1, 8):
        exchange_z(0, k).start()

    gather(0).wait_recv()
    gather(3).start()
    gather(1).wait_recv()
    gather(4).start()
    gather(2).wait_recv()
    gather(5).start()

    head(1)
    for k in range(3):
        gpt[k] = gp[k].T

    gather(3).wait_recv()
    gather(6).start()
    gather(4).wait_recv()
    gather(7).start()
    gather(5).wait_recv()
    gather(8).start()

    for k in range(1, 8):
        exchange_z(0, k).wait_recv()
    centers = [sz_send[0, 0:4, :]] + [sz_recv[0, k, 0:4, :] for k in range(1, 8)]
    squares = [sz_send[0, 4:8, :]] + [sz_recv[0, k, 4:8, :] for k in range(1, 8)]
    center = sum(centers) * 0.125
    spread = (sum(squares) + (2 * COLS) * sum(jnp.square(one - center) for one in centers)) / D
    spread_rows(center, mean_b)
    spread_rows(lax.rsqrt(spread + 1e-06), inv_b)

    def owner(n):
        m = n % 8
        dz = ((m + 1) // 2) * (1 - 2 * (m % 2))
        return ((z + dz + 8) % 8) * 2 + (x + n // 8) % 2

    loads[3].wait()

    def share(n, carry):
        first = pl.multiple_of(owner(n) * COLS, COLS)
        total = dot(gp[0], wv[0, pl.ds(first, COLS), :], NT)
        total = total + dot(gp[1], wv[1, pl.ds(first, COLS), :], NT)
        total = total + dot(gp[2], wv[2, pl.ds(first, COLS), :], NT)
        part[n] = total.astype(BF16)
        return carry

    lax.fori_loop(0, 16, share, 0)

    gather(6).wait_recv()
    gather(9).start()
    gather(7).wait_recv()
    gather(10).start()
    gather(8).wait_recv()
    gather(12).start()
    gather(11).start()

    acc_a[...] = jnp.zeros_like(acc_a)
    acc_b[...] = jnp.zeros_like(acc_b)

    def reduce_half(sign, dx):
        n = (0 if sign > 0 else 1) + 2 * dx
        half = 1 if sign > 0 else 0
        src = part.at[slot(4, dx), pl.ds(half * HALF, HALF)]
        return remote(src, halves.at[n], rs_s.at[13 + n], rs_r.at[13 + n], at_z(sign))

    def reduce_z(sign, k, dx):
        n = {(3, 1): 0, (3, 0): 2, (2, 0): 4, (1, 0): 6}[(k, dx)] + (0 if sign > 0 else 1)
        return remote(part.at[slot(sign * k, dx)], landed.at[n], rs_s.at[n], rs_r.at[n], at_z(sign))

    def reduce_x(dz):
        n = {1: 8, -1: 9, 2: 10, -2: 11, 0: 12}[dz]
        return remote(part.at[slot(dz, 1)], landed.at[n], rs_s.at[n], rs_r.at[n], at_x)

    def block_index(dy, dxh, dc):
        return ((y + dy) % 4) * 4 + ((xh + dxh) % 2) * 2 + (c + dc) % 2

    def core_copy(j, k):
        return remote(gsum.at[j], cland.at[k], c_s.at[k], c_r.at[k], at_c)

    def weight(i, carry):
        q = i % 8
        cross = q + (q + 6) // 8 - 4 * ((q + 3) // 8) + 3 * ((q + 2) // 8)
        n = i + (i // 8) * (cross - q)

        @pl.when(i == 7)
        def _():
            gather(9).wait_recv()
            gather(10).wait_recv()

        @pl.when(i == 8)
        def _():
            gather(11).wait_recv()
            gather(14).start()
            gather(13).start()

        @pl.when(i == 12)
        def _():
            gather(12).wait_recv()
            gather(15).start()

        @pl.when(i == 13)
        def _():
            gather(14).wait_recv()
            gather(16).start()
            gather(13).wait_recv()
            reduce_x(1).start()

        @pl.when(i == 15)
        def _():
            gather(15).wait_recv()
            gather(16).wait_recv()
            reduce_half(1, 1).start()
            reduce_half(-1, 1).start()

        j = owner(n)

        def rows_step(r, carry):
            rows = pl.ds(pl.multiple_of(r * 64, 64), 64)
            center, inverse = mean_b[rows, :], inv_b[rows, :]
            plain, hat = acc_a[rows, :], acc_b[rows, :]
            for k in range(3):
                lanes = slice(k * LANES, (k + 1) * LANES)
                scale = gain[j, :, lanes]
                value = (ag[n, rows, lanes].astype(F32) - center) * inverse * scale
                normed[rows, lanes] = value.astype(BF16)
                piece = part[n, rows, lanes].astype(F32)
                plain = plain + piece * scale
                hat = hat + piece * value
            acc_a[rows, :] = plain
            acc_b[rows, :] = hat
            return carry

        lax.fori_loop(0, SEQ // 64, rows_step, 0)
        for k in range(3):
            gsum[j, k * WIDTH : (k + 1) * WIDTH, :] = dot(gpt[k], normed[...], NN).astype(BF16)

        @pl.when((j + c) % 2 == 1)
        def _():
            core_copy(j, ((j // 4 - y + 4) % 4) * 2 + (j // 2 + xh) % 2).start()

        return carry

    lax.fori_loop(0, 16, weight, 0)

    pack_rows(acc_a, st_send.at[1], 0)
    pack_rows(acc_b, st_send.at[1], 4)
    exchange_x(1).start()

    def core_add(dy, dxh):
        k = dy * 2 + dxh
        core_copy(0, k).wait_recv()
        add_into(cland.at[k], [gsum.at[block_index(dy, dxh, 0)]], GROWS)

    def y_half(sign, dxh):
        n = dxh * 2 + (0 if sign > 0 else 1)
        half = 0 if sign > 0 else 1
        src = cland.at[4 + dxh, pl.ds(half * GHALF, GHALF)]
        return remote(src, yhalf.at[n], y_s.at[n], y_r.at[n], at_y(sign))

    def y_full(sign, dxh):
        n = dxh * 2 + (0 if sign > 0 else 1)
        src = cland.at[(2 if sign > 0 else 6) + dxh]
        return remote(src, yland.at[n], y_s.at[4 + n], y_r.at[4 + n], at_y(sign))

    def y_pass(dxh):
        for sign, dy, half in ((1, 1, 0), (-1, 3, 1)):
            n = dxh * 2 + (0 if sign > 0 else 1)
            y_half(sign, dxh).wait_recv()
            add_into(cland.at[dy * 2 + dxh, pl.ds(half * GHALF, GHALF)], [yhalf.at[n]], GHALF)
            y_full(sign, dxh).start()

    x_copy = remote(cland.at[1], xland, y_s.at[8], y_r.at[8], at_xh)

    core_add(2, 1)
    y_half(1, 1).start()
    y_half(-1, 1).start()
    core_add(1, 1)
    core_add(3, 1)

    for sign, n in ((1, 2), (-1, 3)):
        reduce_half(sign, 1).wait_recv()
        half = 1 if sign > 0 else 0
        add_into(part.at[slot(3 * sign, 1), pl.ds(half * HALF, HALF)], [halves.at[n]], HALF)
        reduce_z(sign, 3, 1).start()
    reduce_x(-1).start()

    exchange_x(1).wait_recv()
    sz_send[1] = st_send[1] + st_recv[1]
    for k in range(1, 8):
        exchange_z(1, k).start()

    y_pass(1)
    core_add(2, 0)
    core_add(0, 1)
    core_add(1, 0)
    core_add(3, 0)
    core_add(0, 0)

    for sign, n in ((1, 0), (-1, 1)):
        reduce_z(sign, 3, 1).wait_recv()
        add_into(part.at[slot(2 * sign, 1)], [landed.at[n]], SEQ)
        reduce_x(2 * sign).start()
        reduce_half(sign, 0).start()

    for k in range(1, 8):
        exchange_z(1, k).wait_recv()
    sums = (sz_send[1] + sum(sz_recv[1, k] for k in range(1, 8))) / D
    spread_rows(sums[0:4], acc_a)
    spread_rows(sums[4:8], acc_b)

    for sign, n in ((1, 0), (-1, 1)):
        reduce_half(sign, 0).wait_recv()
        half = 1 if sign > 0 else 0
        add_into(part.at[slot(3 * sign, 0), pl.ds(half * HALF, HALF)], [halves.at[n]], HALF)
        reduce_z(sign, 3, 0).start()

    y_full(1, 1).wait_recv()
    y_full(-1, 1).wait_recv()
    y_half(1, 0).start()
    y_half(-1, 0).start()
    add_into(cland.at[1], [yland.at[2], yland.at[3]], GROWS)
    x_copy.start()

    for sign, n in ((1, 0), (-1, 1)):
        reduce_z(sign, 3, 0).wait_recv()
        reduce_x(2 * sign).wait_recv()
        add_into(part.at[slot(2 * sign, 0)], [landed.at[2 + n], landed.at[10 + n]], SEQ)
        reduce_z(sign, 2, 0).start()
    reduce_x(0).start()

    y_pass(0)

    for sign, n in ((1, 0), (-1, 1)):
        reduce_z(sign, 2, 0).wait_recv()
        reduce_x(sign).wait_recv()
        add_into(part.at[slot(sign, 0)], [landed.at[4 + n], landed.at[8 + n]], SEQ)
        reduce_z(sign, 1, 0).start()

    y_full(1, 0).wait_recv()
    y_full(-1, 0).wait_recv()
    x_copy.wait_recv()
    for k in range(3):

        def out_step(r, carry, k=k):
            rows = pl.ds(pl.multiple_of(k * WIDTH + r * LANES, LANES), LANES)
            total = cland[0, rows, :].astype(F32) + xland[rows, :].astype(F32)
            total = total + yland[0, rows, :].astype(F32) + yland[1, rows, :].astype(F32)
            gw_out[k, :, pl.ds(pl.multiple_of(r * LANES, LANES), LANES)] = total.T
            return carry

        lax.fori_loop(0, WIDTH // LANES, out_step, 0)

    reduce_z(1, 1, 0).wait_recv()
    reduce_z(-1, 1, 0).wait_recv()
    reduce_x(0).wait_recv()

    def in_step(r, carry):
        rows = pl.ds(pl.multiple_of(r * 64, 64), 64)
        center, inverse = mean_b[rows, :], inv_b[rows, :]
        plain, hat = acc_a[rows, :], acc_b[rows, :]
        for k in range(3):
            lanes = slice(k * LANES, (k + 1) * LANES)
            total = part[0, rows, lanes].astype(F32) + landed[6, rows, lanes].astype(F32)
            total = total + landed[7, rows, lanes].astype(F32) + landed[12, rows, lanes].astype(F32)
            x_hat = (ag[0, rows, lanes].astype(F32) - center) * inverse
            scaled = total * gain[mp, :, lanes]
            gi_out[rows, lanes] = ((scaled - plain - x_hat * hat) * inverse).astype(BF16)
        return carry

    lax.fori_loop(0, SEQ // 64, in_step, 0)

    for e in range(len(GATHER)):
        gather(e).wait_send()
    for n in range(2):
        exchange_x(n).wait_send()
        for k in range(1, 8):
            exchange_z(n, k).wait_send()
    for k in range(8):
        core_copy(0, k).wait_send()
    x_copy.wait_send()
    for dz in (1, -1, 2, -2, 0):
        reduce_x(dz).wait_send()
    for sign in (1, -1):
        for n in (0, 1):
            reduce_half(sign, n).wait_send()
            y_half(sign, n).wait_send()
            y_full(sign, n).wait_send()
        for k, dx in ((3, 1), (3, 0), (2, 0), (1, 0)):
            reduce_z(sign, k, dx).wait_send()


def shards(tokens, ln_gain, projected, out_grad, w_joined):
    vmem = pltpu.VMEM
    dma = pltpu.SemaphoreType.DMA
    hbm = pl.BlockSpec(memory_space=pl.ANY)
    local = pl.BlockSpec(memory_space=pltpu.VMEM)
    grad_weight, grad_input = pl.pallas_call(
        kernel,
        out_shape=(
            jax.ShapeDtypeStruct((3, COLS, WIDTH), F32),
            jax.ShapeDtypeStruct((SEQ, COLS), BF16),
        ),
        in_specs=[hbm, local, hbm, hbm, hbm],
        out_specs=(local, local),
        scratch_shapes=[
            vmem((16, SEQ, COLS), BF16),
            vmem((3, D, WIDTH), BF16),
            vmem((3, SEQ, WIDTH), BF16),
            vmem((SEQ, WIDTH), BF16),
            vmem((3, SEQ, WIDTH), BF16),
            vmem((3, WIDTH, SEQ), BF16),
            vmem((16, SEQ, COLS), BF16),
            vmem((4, HALF, COLS), BF16),
            vmem((13, SEQ, COLS), BF16),
            vmem((16, GROWS, COLS), BF16),
            vmem((8, GROWS, COLS), BF16),
            vmem((4, GROWS, COLS), BF16),
            vmem((4, GHALF, COLS), BF16),
            vmem((GROWS, COLS), BF16),
            vmem((SEQ, COLS), BF16),
            vmem((SEQ, LANES), F32),
            vmem((SEQ, LANES), F32),
            vmem((SEQ, LANES), F32),
            vmem((SEQ, LANES), F32),
            vmem((2, 8, LANES), F32),
            vmem((2, 8, LANES), F32),
            vmem((2, 8, LANES), F32),
            vmem((2, 8, 8, LANES), F32),
            dma((4,)),
            dma((17,)), dma((17,)),
            dma((2,)), dma((2,)),
            dma((2, 8)), dma((2, 8)),
            dma((17,)), dma((17,)),
            dma((8,)), dma((8,)),
            dma((9,)), dma((9,)),
        ],
        compiler_params=pltpu.CompilerParams(
            collective_id=0, has_side_effects=True, vmem_limit_bytes=62 * 1024 * 1024
        ),
        cost_estimate=pl.CostEstimate(flops=11_000_000_000, bytes_accessed=14_000_000, transcendentals=600_000),
        name="parallel_block_backward",
    )(
        tokens,
        ln_gain.reshape(16, 1, COLS),
        jnp.transpose(projected, (1, 0, 2)),
        out_grad,
        jnp.transpose(w_joined, (1, 0, 2)),
    )
    return jnp.transpose(grad_weight, (1, 0, 2)), grad_input


def solution(mesh):
    in_specs = (P("dp", "mp"), P(), P("dp", None, "mp"), P("dp", "mp"), P(None, None, "mp"))
    out_specs = (P("dp", None, "mp"), P("dp", "mp"))
    return jax.shard_map(shards, mesh=mesh, in_specs=in_specs, out_specs=out_specs, check_vma=False)
```

time: 554 us -> 125 us (0.23)
  the two profiles are of different devices: /device:TPU:1 before, /device:TPU:8 now
where the time goes in v1:
time: 125 us
  Pallas kernels  121 us (97%)
  local copies, waits for them, and re-layouts  3.16 us (3%)
    pallas_call x1, Pallas kernels, shards(): pl.pallas_call(kernel, out_shape=(jax.ShapeDtypeStruct((3, COLS, WIDTH),...  121 us
    unnamed x4, local copies, waits for them, and re-layouts  3.16 us

profile of v1, /device:TPU:8, one launch (start us, length us, event | category | flops | bytes accessed | tf_op | source)
XLA Modules:
  0.0 124.8 jit_solution(13620736438573132437)
XLA Ops:
  0.6 121.0 %parallel_block_backward.1 = (f32[3,384,256]{2,1,0:T(8,128)}, bf16[512,384]{1,0:T(8,128)(2,1)}) custom-call(bf16[512,384]{1,0:T(8,128)(2,1)} %tok.1, f32[16,1,384]{2,1,0:T(1,128)} %bitcast.7, bf16[3,512,256]{2,1,0:T(8,128)(2,1)} %bitcast.6, bf16[512,256]{1,0:T(8,128)(2,1)} %og.1, bf16[3,6144,256]{2,1,0:T(8,128)(2,1)} %bitcast.5), custom_call_target="tpu_custom_call" | custom-call | flops 11000000512 | bytes 14000000 | tf_op jit(solution)/shard_map/parallel_block_backward/pallas_call | solution.py:476
  121.6 0.0 copy-start
  121.6 2.4 %copy.9 = f32[384,3,256]{2,0,1:T(8,128)} copy(f32[384,3,256]{2,0,1:T(8,128)} %bitcast.4) | data formatting | bytes 2359296
  124.0 0.0 copy-done
  124.0 0.7 copy.10
Async XLA Ops:
  121.6 2.4 %copy-start = (bf16[512,384]{1,0:T(8,128)(2,1)S(1)}, bf16[512,384]{1,0:T(8,128)(2,1)}, u32[]{:S(2)}) copy-start(bf16[512,384]{1,0:T(8,128)(2,1)} %get-tuple-element.9) | copy-start | bytes 1179652

commit v2 on v0

v2 whole, which is shorter than its diff:
```python
import functools

import jax
import jax.numpy as jnp
from jax import lax
from jax.experimental import pallas as pl
from jax.experimental.pallas import tpu as pltpu
from jax.sharding import PartitionSpec as P

MESH = pl.DeviceIdType.MESH
F32 = jnp.float32
BF16 = jnp.bfloat16

D = 6144
HDIM = 128
SEQ = 512
COLS = 384
WIDTH = 256
HALF = SEQ // 2
GCOLS = 3 * HDIM
GHALF = GCOLS // 2
SCALE = HDIM ** (-0.5)
LANES = 128

NT = (((1,), (1,)), ((), ()))
NN = (((1,), (0,)), ((), ()))
TN = (((0,), (0,)), ((), ()))


def slot(dz):
    return 7 if abs(dz) == 4 else (2 * abs(dz) - (1 if dz < 0 else 0))


def dot(left, right, dims):
    return lax.dot_general(left, right, dims, preferred_element_type=F32)


def add_into(dst, sources, rows, chunk=64):
    def body(i, carry):
        at = pl.ds(pl.multiple_of(i * chunk, chunk), chunk)
        total = dst[at, :].astype(F32)
        for source in sources:
            total = total + source[at, :].astype(F32)
        dst[at, :] = total.astype(BF16)
        return carry

    lax.fori_loop(0, rows // chunk, body, 0)


def pack_rows(acc, out, first):
    for i in range(4):
        part = acc[i * LANES : (i + 1) * LANES, :]
        out[first + i : first + i + 1, :] = jnp.sum(part.T, axis=0, keepdims=True)


def spread_rows(rows, out):
    for i in range(4):
        out[i * LANES : (i + 1) * LANES, :] = jnp.broadcast_to(rows[i : i + 1, :], (LANES, LANES)).T


def kernel(
    tok, gain, proj, og, w, gw_out, gi_out,
    ag, wv, wx, pv, ov, gp, gpt, norm, part, rland, gsum, cland, yland, yhalf, xland, fin, last,
    acc_a, acc_b, mean_b, inv_b, st_send, st_recv, sz_send, sz_recv,
    load_sem, w_sem, ag_s, ag_r, st_s, st_r, sz_s, sz_r, wx_s, wx_r, wc_s, wc_r, gp_s, gp_r,
    rs_s, rs_r, c_s, c_r, y_s, y_r, x_s, x_r, f_s, f_r,
):
    dp, mp = lax.axis_index("dp"), lax.axis_index("mp")
    y, xh, c = dp // 4, (dp // 2) % 2, dp % 2
    z, x = mp // 2, mp % 2

    def at_z(k):
        return (dp, ((z + k + 8) % 8) * 2 + x)

    def at_y(k):
        return (((y + k + 4) % 4) * 4 + xh * 2 + c, mp)

    sibling = y * 4 + xh * 2 + 1 - c
    at_c = (sibling, mp)
    at_x = (dp, z * 2 + 1 - x)
    at_xc = (sibling, z * 2 + 1 - x)
    at_xh = (y * 4 + (1 - xh) * 2 + c, mp)
    at_xo = (y * 4 + (1 - xh) * 2 + c, z * 2 + 1 - x)

    def remote(src, dst, send, recv, device):
        return pltpu.make_async_remote_copy(
            src_ref=src, dst_ref=dst, send_sem=send, recv_sem=recv, device_id=device, device_id_type=MESH
        )

    def zed(n):
        return (z + ((n + 1) // 2) * (1 - 2 * (n % 2)) + 8) % 8

    def w_rows(n, column):
        return w.at[:, pl.ds(pl.multiple_of((zed(n) * 2 + column) * COLS, COLS), COLS), :]

    loads = [
        pltpu.make_async_copy(tok, ag.at[0], load_sem.at[0]),
        pltpu.make_async_copy(proj, pv, load_sem.at[1]),
        pltpu.make_async_copy(og, ov, load_sem.at[2]),
    ]
    for load in loads:
        load.start()

    def w_load(n):
        return pltpu.make_async_copy(w_rows(n, x), wv.at[n], w_sem.at[n])

    barrier = pltpu.get_barrier_semaphore()
    peers = [at_z(k) for k in range(1, 8)] + [at_c, at_x, at_xc, at_xh, at_xo, at_y(1), at_y(-1)]
    for peer in peers:
        pl.semaphore_signal(barrier, inc=1, device_id=peer, device_id_type=MESH)
    pl.semaphore_wait(barrier, len(peers))

    def gather(sign, k):
        hop = (k - 1) // 2
        half = (0 if sign > 0 else 1) if k % 2 == 1 else (1 if sign > 0 else 0)
        rows = pl.ds(half * HALF, HALF)
        src = tok.at[rows] if hop == 0 else ag.at[slot(-sign * hop), rows]
        e = (0 if sign > 0 else 7) + k - 1
        return remote(src, ag.at[slot(-sign * (hop + 1)), rows], ag_s.at[e], ag_r.at[e], at_z(sign))

    def gather_event(k):
        for sign in (1, -1):
            gather(sign, k).wait_recv()
            if k <= 5:
                gather(sign, k + 2).start()

    for k in (1, 2):
        gather(1, k).start()
        gather(-1, k).start()

    def w_place(d, core):
        return 2 * ((y - d + 4) % 4) + 1 - core

    def w_cross():
        n = w_place(0, c)
        partner = (y * 4 + ((xh + c) % 2) * 2 + c, z * 2 + 1 - x)
        return remote(w_rows(n, 1 - x), wx.at[n], wx_s.at[0], wx_r.at[0], partner)

    def w_ring(sign):
        n = w_place(0, c)
        e = 1 if sign > 0 else 2
        return remote(wx.at[n], wx.at[n], wx_s.at[e], wx_r.at[e], at_y(sign))

    def w_ring_far(sign):
        n = w_place(sign, c)
        e = 3 if sign > 0 else 4
        rows = pl.ds(0 if sign > 0 else COLS // 2, COLS // 2)
        return remote(wx.at[n, :, rows], wx.at[n, :, rows], wx_s.at[e], wx_r.at[e], at_y(sign))

    def w_core(i):
        n = w_place((0, 1, -1, 2)[i], c)
        return remote(wx.at[n], wx.at[n], wc_s.at[i], wc_r.at[i], at_c)

    w_cross().start()
    for n in (7, 6, 5, 4, 3, 2, 1, 0):
        w_load(n).start()

    def exchange_x(n):
        return remote(st_send.at[n], st_recv.at[n], st_s.at[n], st_r.at[n], at_x)

    def exchange_z(n, k):
        return remote(sz_send.at[n], sz_recv.at[n, k], sz_s.at[n, k], sz_r.at[n, k], at_z(k))

    loads[0].wait()
    for i in range(4):
        rows = slice(i * LANES, (i + 1) * LANES)
        tiles = [ag[0, rows, k * LANES : (k + 1) * LANES].astype(F32) for k in range(3)]
        sums = tiles[0] + tiles[1] + tiles[2]
        center = jnp.sum(sums, axis=1, keepdims=True) / COLS
        acc_a[rows, :] = sums
        acc_b[rows, :] = sum(jnp.square(tile - center) for tile in tiles)
    pack_rows(acc_a, st_send.at[0], 0)
    pack_rows(acc_b, st_send.at[0], 4)
    st_send[0, 0:4, :] = st_send[0, 0:4, :] / COLS
    exchange_x(0).start()

    def gp_copy(h):
        lanes = pl.ds(h * HDIM, HDIM)
        return remote(gp.at[0, :, :, lanes], gp.at[1, :, :, lanes], gp_s.at[h], gp_r.at[h], at_x)

    def head(h):
        cols = slice(h * HDIM, (h + 1) * HDIM)
        queries, keys_all, values, upstream = pv[0, :, cols], pv[1, :, cols], pv[2, :, cols], ov[:, cols]
        key_grad = value_grad = None
        for q0 in range(0, SEQ, 256):
            qs = slice(q0, q0 + 256)
            scores = dot(keys_all, queries[qs], NT) * SCALE
            raised = jnp.exp(scores - jnp.max(scores, axis=0, keepdims=True))
            probs = raised / jnp.sum(raised, axis=0, keepdims=True)
            term = dot(probs.astype(BF16), upstream[qs], NN)
            value_grad = term if value_grad is None else value_grad + term
            prob_grad = dot(values, upstream[qs], NT)
            score_grad = probs * (prob_grad - jnp.sum(probs * prob_grad, axis=0, keepdims=True))
            score_low = score_grad.astype(BF16)
            term = dot(score_low, queries[qs], NN)
            key_grad = term if key_grad is None else key_grad + term
            gp[0, 0, qs, cols] = (dot(score_low, keys_all, TN) * SCALE).astype(BF16)
        gp[0, 1, :, cols] = (key_grad * SCALE).astype(BF16)
        gp[0, 2, :, cols] = value_grad.astype(BF16)
        gp_copy(h).start()

    def turn(s, h):
        for k in range(3):
            gpt[s, h, k * HDIM : (k + 1) * HDIM, :] = gp[s, k, :, h * HDIM : (h + 1) * HDIM].T

    loads[1].wait()
    loads[2].wait()
    head(0)

    exchange_x(0).wait_recv()
    mine, other = st_send[0], st_recv[0]
    center = (mine[0:4] + other[0:4]) * 0.5
    sz_send[0, 0:4, :] = center
    sz_send[0, 4:8, :] = mine[4:8] + other[4:8] + COLS * (
        jnp.square(mine[0:4] - center) + jnp.square(other[0:4] - center)
    )
    for k in range(1, 8):
        exchange_z(0, k).start()

    gather_event(1)
    w_cross().wait_recv()
    w_ring(1).start()
    w_ring(-1).start()
    w_core(0).start()
    gather_event(2)

    head(1)

    gather_event(3)
    turn(0, 0)
    turn(0, 1)

    for k in range(1, 8):
        exchange_z(0, k).wait_recv()
    centers = [sz_send[0, 0:4, :]] + [sz_recv[0, k, 0:4, :] for k in range(1, 8)]
    squares = [sz_send[0, 4:8, :]] + [sz_recv[0, k, 4:8, :] for k in range(1, 8)]
    center = sum(centers) * 0.125
    spread = (sum(squares) + (2 * COLS) * sum(jnp.square(one - center) for one in centers)) / D
    spread_rows(center, mean_b)
    spread_rows(lax.rsqrt(spread + 1e-06), inv_b)
    gather_event(4)

    acc_a[...] = jnp.zeros_like(acc_a)
    acc_b[...] = jnp.zeros_like(acc_b)

    def core_copy(s, o):
        return remote(gsum.at[s, o, 1 - c], cland.at[s, o], c_s.at[s, o], c_r.at[s, o], at_c)

    def weight(s, n):
        o = ((zed(n) // 2 - y + 4) % 4) * 2 + (zed(n) + xh) % 2
        for h in range(2):
            gsum[s, o, h] = dot(gpt[s, h], norm[n], NN).astype(BF16)
        core_copy(s, o).start()

    def weight_own(n, carry):
        j = zed(n) * 2 + x

        def rows_step(r, carry):
            rows = pl.ds(pl.multiple_of(r * 64, 64), 64)
            center, inverse = mean_b[rows, :], inv_b[rows, :]
            for k in range(3):
                lanes = slice(k * LANES, (k + 1) * LANES)
                value = (ag[n, rows, lanes].astype(F32) - center) * inverse * gain[j, :, lanes]
                norm[n, rows, lanes] = value.astype(BF16)
            return carry

        lax.fori_loop(0, SEQ // 64, rows_step, 0)
        weight(0, n)
        return carry

    def weight_cross(n, carry):
        weight(1, n)
        return carry

    def share(n):
        for k in range(3):
            term = dot(gp[0, k], wv[n, k], NT) + dot(gp[1, k], wx[n, k], NT)
            total = term if k == 0 else total + term
        part[n] = total.astype(BF16)

    def sums(n):
        j = zed(n) * 2 + x

        def rows_step(r, carry):
            rows = pl.ds(pl.multiple_of(r * 64, 64), 64)
            plain, hat = acc_a[rows, :], acc_b[rows, :]
            for k in range(3):
                lanes = slice(k * LANES, (k + 1) * LANES)
                piece = part[n, rows, lanes].astype(F32)
                plain = plain + piece * gain[j, :, lanes]
                hat = hat + piece * norm[n, rows, lanes].astype(F32)
            acc_a[rows, :] = plain
            acc_b[rows, :] = hat
            return carry

        lax.fori_loop(0, SEQ // 64, rows_step, 0)

    def share_far(i, carry):
        share(7 - i)
        return carry

    def share_near(i, carry):
        share(4 - i)
        sums(4 - i)
        return carry

    def sums_far(i, carry):
        sums(7 - i)
        return carry

    def reduce(sign, k):
        dz = sign * (4 - k // 2)
        first = 1 if sign > 0 else 0
        half = first if k % 2 == 1 else 1 - first
        e = (0 if sign > 0 else 7) + k - 1
        return remote(
            part.at[slot(dz), pl.ds(half * HALF, HALF)], rland.at[e], rs_s.at[e], rs_r.at[e], at_z(sign)
        )

    def reduce_event(k):
        for sign in (1, -1):
            dz = sign * (4 - (k + 2) // 2)
            first = 1 if sign > 0 else 0
            half = first if k % 2 == 1 else 1 - first
            reduce(sign, k).wait_recv()
            e = (0 if sign > 0 else 7) + k - 1
            add_into(part.at[slot(dz), pl.ds(half * HALF, HALF)], [rland.at[e]], HALF)
            reduce(sign, k + 2).start()

    lax.fori_loop(0, 3, weight_own, 0)
    gather_event(5)
    for sign in (1, -1):
        w_ring(sign).wait_recv()
        w_ring_far(sign).start()
    w_core(1).start()
    w_core(2).start()
    lax.fori_loop(3, 5, weight_own, 0)
    gp_copy(0).wait_recv()
    gp_copy(1).wait_recv()
    turn(1, 0)
    turn(1, 1)
    gather_event(6)
    lax.fori_loop(5, 7, weight_own, 0)

    w_ring_far(1).wait_recv()
    w_ring_far(-1).wait_recv()
    w_core(3).start()
    for n in range(8):
        w_load(n).wait()
    for i in range(4):
        w_core(i).wait_recv()
    lax.fori_loop(0, 3, share_far, 0)
    for k in (1, 2):
        reduce(1, k).start()
        reduce(-1, k).start()

    gather_event(7)
    lax.fori_loop(7, 8, weight_own, 0)
    lax.fori_loop(0, 3, sums_far, 0)

    def core_add(s, dy, dxh, more=()):
        o = dy * 2 + dxh
        core_copy(s, o).wait_recv()
        add_into(cland.at[s, o], [gsum.at[s, o, c], *more], GCOLS)

    def y_place(s, sign, dxh):
        return s * 4 + dxh * 2 + (0 if sign > 0 else 1)

    def y_half(s, sign, dxh):
        n = y_place(s, sign, dxh)
        half = 0 if sign > 0 else 1
        src = cland.at[s, 4 + dxh, pl.ds(half * GHALF, GHALF)]
        return remote(src, yhalf.at[n], y_s.at[n], y_r.at[n], at_y(sign))

    def y_full(s, sign, dxh):
        n = y_place(s, sign, dxh)
        src = cland.at[s, (2 if sign > 0 else 6) + dxh]
        return remote(src, yland.at[n], y_s.at[8 + n], y_r.at[8 + n], at_y(sign))

    def y_pass(s, dxh):
        for sign, dy, half in ((1, 1, 0), (-1, 3, 1)):
            n = y_place(s, sign, dxh)
            y_half(s, sign, dxh).wait_recv()
            add_into(cland.at[s, dy * 2 + dxh, pl.ds(half * GHALF, GHALF)], [yhalf.at[n]], GHALF)
            y_full(s, sign, dxh).start()

    def x_copy(n):
        src = cland.at[1, 1] if n == 4 else cland.at[0, n * 2 + 1]
        return remote(src, xland.at[n], x_s.at[n], x_r.at[n], at_xh)

    for dy in (2, 1):
        core_add(0, dy, 1)
        x_copy(dy).start()

    lax.fori_loop(0, 8, weight_cross, 0)
    core_add(1, 2, 1)
    y_half(1, 1, 1).start()
    y_half(1, -1, 1).start()
    reduce_event(1)
    core_add(1, 2, 0)
    y_half(1, 1, 0).start()
    y_half(1, -1, 0).start()
    core_add(0, 3, 1)
    x_copy(3).start()
    core_add(1, 1, 1)
    core_add(1, 3, 1)
    lax.fori_loop(0, 2, share_near, 0)
    y_pass(1, 1)
    reduce_event(2)
    lax.fori_loop(2, 5, share_near, 0)

    pack_rows(acc_a, st_send.at[1], 0)
    pack_rows(acc_b, st_send.at[1], 4)
    exchange_x(1).start()

    reduce_event(3)
    core_add(0, 0, 1)
    x_copy(0).start()
    core_add(1, 1, 0)
    core_add(1, 3, 0)
    y_pass(1, 0)
    exchange_x(1).wait_recv()
    sz_send[1] = st_send[1] + st_recv[1]
    for k in range(1, 8):
        exchange_z(1, k).start()
    core_add(1, 0, 1)
    core_add(1, 0, 0)
    reduce_event(4)

    y_full(1, 1, 1).wait_recv()
    y_full(1, -1, 1).wait_recv()
    add_into(cland.at[1, 1], [yland.at[6], yland.at[7]], GCOLS)
    x_copy(4).start()
    x_copy(2).wait_recv()
    core_add(0, 2, 0, [xland.at[2]])
    y_half(0, 1, 0).start()
    y_half(0, -1, 0).start()
    reduce_event(5)

    for dy in (1, 3):
        x_copy(dy).wait_recv()
        core_add(0, dy, 0, [xland.at[dy]])

    for k in range(1, 8):
        exchange_z(1, k).wait_recv()
    total = (sz_send[1] + sum(sz_recv[1, k] for k in range(1, 8))) / D
    spread_rows(total[0:4], acc_a)
    spread_rows(total[4:8], acc_b)

    owner_b = (y * 4 + xh * 2 + x, z * 2 + 1 - x)
    copy_b = remote(last.at[1], fin.at[c], f_s.at[1], f_r.at[c], owner_b)
    copy_a = remote(last.at[0], fin.at[c], f_s.at[0], f_r.at[c], at_c)

    def finish(s, sources):
        def step(r, carry):
            rows = pl.ds(pl.multiple_of(r * 64, 64), 64)
            total = cland[s, 0, rows, :].astype(F32)
            for source in sources:
                total = total + source[rows, :].astype(F32)
            last[s, rows, :] = total.astype(BF16)
            return carry

        lax.fori_loop(0, GCOLS // 64, step, 0)

    y_full(1, 1, 0).wait_recv()
    y_full(1, -1, 0).wait_recv()
    x_copy(4).wait_recv()
    finish(1, [yland.at[4], yland.at[5], xland.at[4]])
    copy_b.start()
    y_pass(0, 0)
    x_copy(0).wait_recv()
    core_add(0, 0, 0, [xland.at[0]])

    for k in (6, 7):
        reduce(1, k).wait_recv()
        reduce(-1, k).wait_recv()

    def in_step(r, carry):
        center, inverse = None, None
        for half in range(2):
            rows = pl.ds(pl.multiple_of(half * HALF + r * 64, 64), 64)
            inner = pl.ds(pl.multiple_of(r * 64, 64), 64)
            up, down = (5, 13) if half == 0 else (6, 12)
            center, inverse = mean_b[rows, :], inv_b[rows, :]
            plain, hat = acc_a[rows, :], acc_b[rows, :]
            for k in range(3):
                lanes = slice(k * LANES, (k + 1) * LANES)
                total = part[0, rows, lanes].astype(F32) + rland[up, inner, lanes].astype(F32)
                total = total + rland[down, inner, lanes].astype(F32)
                x_hat = (ag[0, rows, lanes].astype(F32) - center) * inverse
                scaled = total * gain[mp, :, lanes]
                gi_out[rows, lanes] = ((scaled - plain - x_hat * hat) * inverse).astype(BF16)
        return carry

    lax.fori_loop(0, HALF // 64, in_step, 0)

    y_full(0, 1, 0).wait_recv()
    y_full(0, -1, 0).wait_recv()
    finish(0, [yland.at[0], yland.at[1]])

    @pl.when(c == x)
    def _():
        fin[c] = last[0]
        remote(last.at[0], fin.at[1 - c], f_s.at[0], f_r.at[1 - c], at_c).wait_recv()

    @pl.when(c != x)
    def _():
        copy_a.start()
        for h in range(2):
            remote(last.at[1], fin.at[h], f_s.at[1], f_r.at[h], at_x).wait_recv()
        copy_a.wait_send()

    for h in range(2):
        for k in range(3):
            block = fin[h, k * HDIM : (k + 1) * HDIM, :].astype(F32)
            gw_out[k, :, h * HDIM : (h + 1) * HDIM] = block.T

    copy_b.wait_send()
    for sign in (1, -1):
        for k in range(1, 8):
            gather(sign, k).wait_send()
            reduce(sign, k).wait_send()
        for s, dxh in ((1, 1), (1, 0), (0, 0)):
            y_half(s, sign, dxh).wait_send()
            y_full(s, sign, dxh).wait_send()
    for n in range(2):
        gp_copy(n).wait_send()
        exchange_x(n).wait_send()
        for k in range(1, 8):
            exchange_z(n, k).wait_send()
        for o in range(8):
            core_copy(n, o).wait_send()
    w_cross().wait_send()
    for sign in (1, -1):
        w_ring(sign).wait_send()
        w_ring_far(sign).wait_send()
    for i in range(4):
        w_core(i).wait_send()
    for n in range(5):
        x_copy(n).wait_send()


def shards(tokens, ln_gain, projected, out_grad, w_joined):
    vmem = pltpu.VMEM
    dma = pltpu.SemaphoreType.DMA
    hbm = pl.BlockSpec(memory_space=pl.ANY)
    local = pl.BlockSpec(memory_space=pltpu.VMEM)
    grad_weight, grad_input = pl.pallas_call(
        kernel,
        out_shape=(
            jax.ShapeDtypeStruct((3, COLS, WIDTH), F32),
            jax.ShapeDtypeStruct((SEQ, COLS), BF16),
        ),
        in_specs=[hbm, local, hbm, hbm, hbm],
        out_specs=(local, local),
        scratch_shapes=[
            vmem((8, SEQ, COLS), BF16),
            vmem((8, 3, COLS, WIDTH), BF16),
            vmem((8, 3, COLS, WIDTH), BF16),
            vmem((3, SEQ, WIDTH), BF16),
            vmem((SEQ, WIDTH), BF16),
            vmem((2, 3, SEQ, WIDTH), BF16),
            vmem((2, 2, GCOLS, SEQ), BF16),
            vmem((8, SEQ, COLS), BF16),
            vmem((8, SEQ, COLS), BF16),
            vmem((14, HALF, COLS), BF16),
            vmem((2, 8, 2, GCOLS, COLS), BF16),
            vmem((2, 8, GCOLS, COLS), BF16),
            vmem((8, GCOLS, COLS), BF16),
            vmem((8, GHALF, COLS), BF16),
            vmem((5, GCOLS, COLS), BF16),
            vmem((2, GCOLS, COLS), BF16),
            vmem((2, GCOLS, COLS), BF16),
            vmem((SEQ, LANES), F32),
            vmem((SEQ, LANES), F32),
            vmem((SEQ, LANES), F32),
            vmem((SEQ, LANES), F32),
            vmem((2, 8, LANES), F32),
            vmem((2, 8, LANES), F32),
            vmem((2, 8, LANES), F32),
            vmem((2, 8, 8, LANES), F32),
            dma((3,)),
            dma((8,)),
            dma((14,)), dma((14,)),
            dma((2,)), dma((2,)),
            dma((2, 8)), dma((2, 8)),
            dma((5,)), dma((5,)),
            dma((4,)), dma((4,)),
            dma((2,)), dma((2,)),
            dma((14,)), dma((14,)),
            dma((2, 8)), dma((2, 8)),
            dma((16,)), dma((16,)),
            dma((5,)), dma((5,)),
            dma((2,)), dma((2,)),
        ],
        compiler_params=pltpu.CompilerParams(
            collective_id=0, has_side_effects=True, vmem_limit_bytes=62 * 1024 * 1024
        ),
        cost_estimate=pl.CostEstimate(flops=11_000_000_000, bytes_accessed=14_000_000, transcendentals=600_000),
        name="parallel_block_backward",
    )(
        tokens,
        ln_gain.reshape(16, 1, COLS),
        jnp.transpose(projected, (1, 0, 2)),
        out_grad,
        jnp.transpose(w_joined, (1, 0, 2)),
    )
    return jnp.transpose(grad_weight, (1, 0, 2)), grad_input


def solution(mesh):
    in_specs = (P("dp", "mp"), P(), P("dp", None, "mp"), P("dp", "mp"), P(None, None, "mp"))
    out_specs = (P("dp", None, "mp"), P("dp", "mp"))
    return jax.shard_map(shards, mesh=mesh, in_specs=in_specs, out_specs=out_specs, check_vma=False)
```

time: 554 us -> 102 us (0.18)
  waiting for transfers between devices: 452 us -> 0 us
  Pallas kernels: 0 us -> 98.3 us
  blocking collectives: 26 us -> 0 us
  other arithmetic: 21.5 us -> 0 us
  matrix products: 19.7 us -> 0 us
  local copies, waits for them, and re-layouts: 20.2 us -> 3.16 us
  between operations: 13.8 us -> 0.65 us
    reduce_scatter x2 -> x0, waiting for transfers between devices: 334 us -> none  [the longest x1 246 us: shards(): lax.psum_scatter(lax.dot_general(sliced, grad_flat, (((1,), (1,)), ((), (...]
    all_gather x1 -> x0, waiting for transfers between devices: 117 us -> none  [shards(): gathered = lax.all_gather(tokens, 'mp', axis=1, tiled=True)]
    pallas_call x0 -> x1, Pallas kernels: none -> 98.3 us  [shards(): pl.pallas_call(kernel, out_shape=(jax.ShapeDtypeStruct((3, COLS, WIDTH),...]
    psum x1 -> x0, blocking collectives: 26 us -> none  [shards(): lax.psum((jnp.sum(scaled, axis=-1), jnp.sum(scaled * hat_share, axis=-1))...]
    dot_general x6 -> x0, matrix products: 18.8 us -> none  [the longest x1 8.71 us: shards(): lax.dot_general(sliced, grad_flat, (((0,), (0,)), ((), ())), preferred_el...]
    unnamed x13 -> x4, local copies, waits for them, and re-layouts: 17.8 us -> 3.16 us
    mul x1 -> x0, other arithmetic: 9.84 us -> none  [normalize(): return ((values - center) * inverse, inverse)]
    reduce_sum x4 -> x0, other arithmetic: 8.42 us -> none  [the longest x1 3.84 us: normalize(): center = jnp.mean(values, axis=-1, keepdims=True)]
  transfers between devices with their start and end apart: 3 -> 0, of which waited for: 3 -> 0; matrix products, arithmetic and copies ran while one was open for 10% -> 0% of each run, Pallas kernels for 0% -> 0%
where the time goes in v2:
time: 102 us
  Pallas kernels  98.3 us (96%)
  local copies, waits for them, and re-layouts  3.16 us (3%)
    pallas_call x1, Pallas kernels, shards(): pl.pallas_call(kernel, out_shape=(jax.ShapeDtypeStruct((3, COLS, WIDTH),...  98.3 us
    unnamed x4, local copies, waits for them, and re-layouts  3.16 us

profile of v2, /device:TPU:1, one launch (start us, length us, event | category | flops | bytes accessed | tf_op | source)
XLA Modules:
  0.0 102.1 jit_solution(412719568992176446)
XLA Ops:
  0.6 98.3 %parallel_block_backward.1 = (f32[3,384,256]{2,1,0:T(8,128)}, bf16[512,384]{1,0:T(8,128)(2,1)}) custom-call(bf16[512,384]{1,0:T(8,128)(2,1)} %tok.1, f32[16,1,384]{2,1,0:T(1,128)} %bitcast.7, bf16[3,512,256]{2,1,0:T(8,128)(2,1)} %bitcast.6, bf16[512,256]{1,0:T(8,128)(2,1)} %og.1, bf16[3,6144,256]{2,1,0:T(8,128)(2,1)} %bitcast.5), custom_call_target="tpu_custom_call" | custom-call | flops 11000000512 | bytes 14000000 | tf_op jit(solution)/shard_map/parallel_block_backward/pallas_call | solution.py:548
  98.9 0.0 copy-start
  98.9 2.4 %copy.9 = f32[384,3,256]{2,0,1:T(8,128)} copy(f32[384,3,256]{2,0,1:T(8,128)} %bitcast.4) | data formatting | bytes 2359296
  101.3 0.0 copy-done
  101.3 0.7 copy.10
Async XLA Ops:
  98.9 2.4 %copy-start = (bf16[512,384]{1,0:T(8,128)(2,1)S(1)}, bf16[512,384]{1,0:T(8,128)(2,1)}, u32[]{:S(2)}) copy-start(bf16[512,384]{1,0:T(8,128)(2,1)} %get-tuple-element.9) | copy-start | bytes 1179652

commit v3 on v2

--- a/solution.py
+++ b/solution.py
@@ -21,6 +21,7 @@
 GHALF = GCOLS // 2
 SCALE = HDIM ** (-0.5)
 LANES = 128
+LAST = None
 
 NT = (((1,), (1,)), ((), ()))
 NN = (((1,), (0,)), ((), ()))
@@ -124,9 +125,8 @@
             if k <= 5:
                 gather(sign, k + 2).start()
 
-    for k in (1, 2):
-        gather(1, k).start()
-        gather(-1, k).start()
+    gather(1, 1).start()
+    gather(-1, 1).start()
 
     def w_place(d, core):
         return 2 * ((y - d + 4) % 4) + 1 - core
@@ -136,10 +136,11 @@
         partner = (y * 4 + ((xh + c) % 2) * 2 + c, z * 2 + 1 - x)
         return remote(w_rows(n, 1 - x), wx.at[n], wx_s.at[0], wx_r.at[0], partner)
 
-    def w_ring(sign):
+    def w_ring(sign, part):
         n = w_place(0, c)
-        e = 1 if sign > 0 else 2
-        return remote(wx.at[n], wx.at[n], wx_s.at[e], wx_r.at[e], at_y(sign))
+        e = (1 if sign > 0 else 2) + 4 * part
+        rows = pl.ds(0 if (sign > 0) == (part == 0) else COLS // 2, COLS // 2)
+        return remote(wx.at[n, :, rows], wx.at[n, :, rows], wx_s.at[e], wx_r.at[e], at_y(sign))
 
     def w_ring_far(sign):
         n = w_place(sign, c)
@@ -173,6 +174,8 @@
     pack_rows(acc_b, st_send.at[0], 4)
     st_send[0, 0:4, :] = st_send[0, 0:4, :] / COLS
     exchange_x(0).start()
+    gather(1, 2).start()
+    gather(-1, 2).start()
 
     def gp_copy(h):
         lanes = pl.ds(h * HDIM, HDIM)
@@ -219,16 +222,21 @@
 
     gather_event(1)
     w_cross().wait_recv()
-    w_ring(1).start()
-    w_ring(-1).start()
+    w_ring(1, 0).start()
+    w_ring(-1, 0).start()
     w_core(0).start()
+
+    head(1)
+
     gather_event(2)
-
-    head(1)
-
-    gather_event(3)
+    w_ring(1, 1).start()
+    w_ring(-1, 1).start()
     turn(0, 0)
     turn(0, 1)
+    gather_event(3)
+    for sign in (1, -1):
+        w_ring(sign, 0).wait_recv()
+        w_ring_far(sign).start()
 
     for k in range(1, 8):
         exchange_z(0, k).wait_recv()
@@ -252,6 +260,20 @@
             gsum[s, o, h] = dot(gpt[s, h], norm[n], NN).astype(BF16)
         core_copy(s, o).start()
 
+    def x_copy(n):
+        src = cland.at[1, 1] if n is LAST else cland.at[0, n * 2 + 1]
+        n = 4 if n is LAST else n
+        return remote(src, xland.at[n], x_s.at[n], x_r.at[n], at_xh)
+
+    def x_event(n):
+        dy = (zed(n) // 2 - y + 4) % 4
+
+        @pl.when((zed(n) + xh) % 2 == 1)
+        def _():
+            core_copy(0, dy * 2 + 1).wait_recv()
+            add_into(cland.at[0, dy * 2 + 1], [gsum.at[0, dy * 2 + 1, c]], GCOLS)
+            x_copy(dy).start()
+
     def weight_own(n, carry):
         j = zed(n) * 2 + x
 
@@ -266,6 +288,11 @@
 
         lax.fori_loop(0, SEQ // 64, rows_step, 0)
         weight(0, n)
+
+        @pl.when(n > 0)
+        def _():
+            x_event(n - 1)
+
         return carry
 
     def weight_cross(n, carry):
@@ -329,9 +356,8 @@
 
     lax.fori_loop(0, 3, weight_own, 0)
     gather_event(5)
-    for sign in (1, -1):
-        w_ring(sign).wait_recv()
-        w_ring_far(sign).start()
+    w_ring(1, 1).wait_recv()
+    w_ring(-1, 1).wait_recv()
     w_core(1).start()
     w_core(2).start()
     lax.fori_loop(3, 5, weight_own, 0)
@@ -341,6 +367,7 @@
     turn(1, 1)
     gather_event(6)
     lax.fori_loop(5, 7, weight_own, 0)
+    lax.fori_loop(0, 5, weight_cross, 0)
 
     w_ring_far(1).wait_recv()
     w_ring_far(-1).wait_recv()
@@ -350,13 +377,15 @@
     for i in range(4):
         w_core(i).wait_recv()
     lax.fori_loop(0, 3, share_far, 0)
-    for k in (1, 2):
-        reduce(1, k).start()
-        reduce(-1, k).start()
+    reduce(1, 1).start()
+    reduce(-1, 1).start()
 
     gather_event(7)
     lax.fori_loop(7, 8, weight_own, 0)
-    lax.fori_loop(0, 3, sums_far, 0)
+    x_event(7)
+    lax.fori_loop(5, 8, weight_cross, 0)
+    reduce(1, 2).start()
+    reduce(-1, 2).start()
 
     def core_add(s, dy, dxh, more=()):
         o = dy * 2 + dxh
@@ -384,24 +413,14 @@
             add_into(cland.at[s, dy * 2 + dxh, pl.ds(half * GHALF, GHALF)], [yhalf.at[n]], GHALF)
             y_full(s, sign, dxh).start()
 
-    def x_copy(n):
-        src = cland.at[1, 1] if n == 4 else cland.at[0, n * 2 + 1]
-        return remote(src, xland.at[n], x_s.at[n], x_r.at[n], at_xh)
-
-    for dy in (2, 1):
-        core_add(0, dy, 1)
-        x_copy(dy).start()
-
-    lax.fori_loop(0, 8, weight_cross, 0)
     core_add(1, 2, 1)
     y_half(1, 1, 1).start()
     y_half(1, -1, 1).start()
+    lax.fori_loop(0, 3, sums_far, 0)
     reduce_event(1)
     core_add(1, 2, 0)
     y_half(1, 1, 0).start()
     y_half(1, -1, 0).start()
-    core_add(0, 3, 1)
-    x_copy(3).start()
     core_add(1, 1, 1)
     core_add(1, 3, 1)
     lax.fori_loop(0, 2, share_near, 0)
@@ -414,8 +433,6 @@
     exchange_x(1).start()
 
     reduce_event(3)
-    core_add(0, 0, 1)
-    x_copy(0).start()
     core_add(1, 1, 0)
     core_add(1, 3, 0)
     y_pass(1, 0)
@@ -430,7 +447,7 @@
     y_full(1, 1, 1).wait_recv()
     y_full(1, -1, 1).wait_recv()
     add_into(cland.at[1, 1], [yland.at[6], yland.at[7]], GCOLS)
-    x_copy(4).start()
+    x_copy(LAST).start()
     x_copy(2).wait_recv()
     core_add(0, 2, 0, [xland.at[2]])
     y_half(0, 1, 0).start()
@@ -464,7 +481,7 @@
 
     y_full(1, 1, 0).wait_recv()
     y_full(1, -1, 0).wait_recv()
-    x_copy(4).wait_recv()
+    x_copy(LAST).wait_recv()
     finish(1, [yland.at[4], yland.at[5], xland.at[4]])
     copy_b.start()
     y_pass(0, 0)
@@ -532,11 +549,12 @@
             core_copy(n, o).wait_send()
     w_cross().wait_send()
     for sign in (1, -1):
-        w_ring(sign).wait_send()
+        w_ring(sign, 0).wait_send()
+        w_ring(sign, 1).wait_send()
         w_ring_far(sign).wait_send()
     for i in range(4):
         w_core(i).wait_send()
-    for n in range(5):
+    for n in (0, 1, 2, 3, LAST):
         x_copy(n).wait_send()
 
 
@@ -584,7 +602,7 @@
             dma((14,)), dma((14,)),
             dma((2,)), dma((2,)),
             dma((2, 8)), dma((2, 8)),
-            dma((5,)), dma((5,)),
+            dma((7,)), dma((7,)),
             dma((4,)), dma((4,)),
             dma((2,)), dma((2,)),
             dma((14,)), dma((14,)),

time: 102 us -> 97.9 us (0.960)
  Pallas kernels: 98.3 us -> 93.9 us
    pallas_call x1, Pallas kernels: 98.3 us -> 93.9 us  [shards(): pl.pallas_call(kernel, out_shape=(jax.ShapeDtypeStruct((3, COLS, WIDTH),...]
where the time goes in v3:
time: 97.9 us; the launch traced here: 97.7 us
  Pallas kernels  93.9 us (96%)
  local copies, waits for them, and re-layouts  3.16 us (3%)
    pallas_call x1, Pallas kernels, shards(): pl.pallas_call(kernel, out_shape=(jax.ShapeDtypeStruct((3, COLS, WIDTH),...  93.9 us
    unnamed x4, local copies, waits for them, and re-layouts  3.16 us

profile of v3, /device:TPU:1, one launch (start us, length us, event | category | flops | bytes accessed | tf_op | source)
XLA Modules:
  0.0 97.7 jit_solution(11011033333086473214)
XLA Ops:
  0.6 93.9 %parallel_block_backward.1 = (f32[3,384,256]{2,1,0:T(8,128)}, bf16[512,384]{1,0:T(8,128)(2,1)}) custom-call(bf16[512,384]{1,0:T(8,128)(2,1)} %tok.1, f32[16,1,384]{2,1,0:T(1,128)} %bitcast.7, bf16[3,512,256]{2,1,0:T(8,128)(2,1)} %bitcast.6, bf16[512,256]{1,0:T(8,128)(2,1)} %og.1, bf16[3,6144,256]{2,1,0:T(8,128)(2,1)} %bitcast.5), custom_call_target="tpu_custom_call" | custom-call | flops 11000000512 | bytes 14000000 | tf_op jit(solution)/shard_map/parallel_block_backward/pallas_call | solution.py:566
  94.5 0.0 copy-start
  94.6 2.4 %copy.9 = f32[384,3,256]{2,0,1:T(8,128)} copy(f32[384,3,256]{2,0,1:T(8,128)} %bitcast.4) | data formatting | bytes 2359296
  97.0 0.0 copy-done
  97.0 0.7 copy.10
Async XLA Ops:
  94.5 2.4 %copy-start = (bf16[512,384]{1,0:T(8,128)(2,1)S(1)}, bf16[512,384]{1,0:T(8,128)(2,1)}, u32[]{:S(2)}) copy-start(bf16[512,384]{1,0:T(8,128)(2,1)} %get-tuple-element.9) | copy-start | bytes 1179652

commit v4 on v3

--- a/solution.py
+++ b/solution.py
@@ -204,7 +204,8 @@
 
     def turn(s, h):
         for k in range(3):
-            gpt[s, h, k * HDIM : (k + 1) * HDIM, :] = gp[s, k, :, h * HDIM : (h + 1) * HDIM].T
+            first = h * GCOLS + k * HDIM
+            gpt[s, first : first + HDIM, :] = gp[s, k, :, h * HDIM : (h + 1) * HDIM].T
 
     loads[1].wait()
     loads[2].wait()
@@ -251,13 +252,15 @@
     acc_a[...] = jnp.zeros_like(acc_a)
     acc_b[...] = jnp.zeros_like(acc_b)
 
+    def head_rows(core):
+        return pl.ds(pl.multiple_of(core * GCOLS, GCOLS), GCOLS)
+
     def core_copy(s, o):
-        return remote(gsum.at[s, o, 1 - c], cland.at[s, o], c_s.at[s, o], c_r.at[s, o], at_c)
+        return remote(gsum.at[s, o, head_rows(1 - c)], cland.at[s, o], c_s.at[s, o], c_r.at[s, o], at_c)
 
     def weight(s, n):
         o = ((zed(n) // 2 - y + 4) % 4) * 2 + (zed(n) + xh) % 2
-        for h in range(2):
-            gsum[s, o, h] = dot(gpt[s, h], norm[n], NN).astype(BF16)
+        gsum[s, o] = dot(gpt[s], norm[n], NN).astype(BF16)
         core_copy(s, o).start()
 
     def x_copy(n):
@@ -271,10 +274,10 @@
         @pl.when((zed(n) + xh) % 2 == 1)
         def _():
             core_copy(0, dy * 2 + 1).wait_recv()
-            add_into(cland.at[0, dy * 2 + 1], [gsum.at[0, dy * 2 + 1, c]], GCOLS)
+            add_into(cland.at[0, dy * 2 + 1], [gsum.at[0, dy * 2 + 1, head_rows(c)]], GCOLS)
             x_copy(dy).start()
 
-    def weight_own(n, carry):
+    def normalize(n):
         j = zed(n) * 2 + x
 
         def rows_step(r, carry):
@@ -287,12 +290,19 @@
             return carry
 
         lax.fori_loop(0, SEQ // 64, rows_step, 0)
+
+    def weight_own(n, carry):
+        normalize(n)
         weight(0, n)
 
-        @pl.when(n > 0)
+        @pl.when(n > 4)
         def _():
             x_event(n - 1)
 
+        return carry
+
+    def x_step(n, carry):
+        x_event(n)
         return carry
 
     def weight_cross(n, carry):
@@ -322,17 +332,13 @@
 
         lax.fori_loop(0, SEQ // 64, rows_step, 0)
 
-    def share_far(i, carry):
-        share(7 - i)
-        return carry
-
     def share_near(i, carry):
         share(4 - i)
         sums(4 - i)
         return carry
 
-    def sums_far(i, carry):
-        sums(7 - i)
+    def sums_step(n, carry):
+        sums(n)
         return carry
 
     def reduce(sign, k):
@@ -363,6 +369,7 @@
     lax.fori_loop(3, 5, weight_own, 0)
     gp_copy(0).wait_recv()
     gp_copy(1).wait_recv()
+    lax.fori_loop(0, 4, x_step, 0)
     turn(1, 0)
     turn(1, 1)
     gather_event(6)
@@ -376,21 +383,22 @@
         w_load(n).wait()
     for i in range(4):
         w_core(i).wait_recv()
-    lax.fori_loop(0, 3, share_far, 0)
+    share(7)
     reduce(1, 1).start()
     reduce(-1, 1).start()
-
+    share(6)
+    reduce(1, 2).start()
+    share(5)
+    reduce(-1, 2).start()
     gather_event(7)
-    lax.fori_loop(7, 8, weight_own, 0)
-    x_event(7)
+    normalize(7)
     lax.fori_loop(5, 8, weight_cross, 0)
-    reduce(1, 2).start()
-    reduce(-1, 2).start()
+    weight(0, 7)
 
     def core_add(s, dy, dxh, more=()):
         o = dy * 2 + dxh
         core_copy(s, o).wait_recv()
-        add_into(cland.at[s, o], [gsum.at[s, o, c], *more], GCOLS)
+        add_into(cland.at[s, o], [gsum.at[s, o, head_rows(c)], *more], GCOLS)
 
     def y_place(s, sign, dxh):
         return s * 4 + dxh * 2 + (0 if sign > 0 else 1)
@@ -416,23 +424,25 @@
     core_add(1, 2, 1)
     y_half(1, 1, 1).start()
     y_half(1, -1, 1).start()
-    lax.fori_loop(0, 3, sums_far, 0)
+    lax.fori_loop(6, 8, x_step, 0)
+    lax.fori_loop(5, 8, sums_step, 0)
     reduce_event(1)
+    lax.fori_loop(0, 2, share_near, 0)
+    reduce_event(2)
     core_add(1, 2, 0)
     y_half(1, 1, 0).start()
     y_half(1, -1, 0).start()
     core_add(1, 1, 1)
     core_add(1, 3, 1)
-    lax.fori_loop(0, 2, share_near, 0)
     y_pass(1, 1)
-    reduce_event(2)
+    reduce_event(3)
     lax.fori_loop(2, 5, share_near, 0)
 
     pack_rows(acc_a, st_send.at[1], 0)
     pack_rows(acc_b, st_send.at[1], 4)
     exchange_x(1).start()
 
-    reduce_event(3)
+    reduce_event(4)
     core_add(1, 1, 0)
     core_add(1, 3, 0)
     y_pass(1, 0)
@@ -442,7 +452,6 @@
         exchange_z(1, k).start()
     core_add(1, 0, 1)
     core_add(1, 0, 0)
-    reduce_event(4)
 
     y_full(1, 1, 1).wait_recv()
     y_full(1, -1, 1).wait_recv()
@@ -529,8 +538,7 @@
 
     for h in range(2):
         for k in range(3):
-            block = fin[h, k * HDIM : (k + 1) * HDIM, :].astype(F32)
-            gw_out[k, :, h * HDIM : (h + 1) * HDIM] = block.T
+            gw_out[k, :, h * HDIM : (h + 1) * HDIM] = fin[h, k * HDIM : (k + 1) * HDIM, :].T
 
     copy_b.wait_send()
     for sign in (1, -1):
@@ -566,7 +574,7 @@
     grad_weight, grad_input = pl.pallas_call(
         kernel,
         out_shape=(
-            jax.ShapeDtypeStruct((3, COLS, WIDTH), F32),
+            jax.ShapeDtypeStruct((3, COLS, WIDTH), BF16),
             jax.ShapeDtypeStruct((SEQ, COLS), BF16),
         ),
         in_specs=[hbm, local, hbm, hbm, hbm],
@@ -578,11 +586,11 @@
             vmem((3, SEQ, WIDTH), BF16),
             vmem((SEQ, WIDTH), BF16),
             vmem((2, 3, SEQ, WIDTH), BF16),
-            vmem((2, 2, GCOLS, SEQ), BF16),
+            vmem((2, 2 * GCOLS, SEQ), BF16),
             vmem((8, SEQ, COLS), BF16),
             vmem((8, SEQ, COLS), BF16),
             vmem((14, HALF, COLS), BF16),
-            vmem((2, 8, 2, GCOLS, COLS), BF16),
+            vmem((2, 8, 2 * GCOLS, COLS), BF16),
             vmem((2, 8, GCOLS, COLS), BF16),
             vmem((8, GCOLS, COLS), BF16),
             vmem((8, GHALF, COLS), BF16),
@@ -623,7 +631,7 @@
         out_grad,
         jnp.transpose(w_joined, (1, 0, 2)),
     )
-    return jnp.transpose(grad_weight, (1, 0, 2)), grad_input
+    return jnp.transpose(grad_weight, (1, 0, 2)).astype(F32), grad_input
 
 
 def solution(mesh):

time: 97.9 us -> 95.4 us (0.974)
  Pallas kernels: 93.9 us -> 90.9 us
  local copies, waits for them, and re-layouts: 3.16 us -> 0.75 us
  other arithmetic: 0 us -> 2.23 us
    pallas_call x1, Pallas kernels: 93.9 us -> 90.9 us  [shards(): pl.pallas_call(kernel, out_shape=(jax.ShapeDtypeStruct((3, COLS, WIDTH),...]
    unnamed x4 -> x3, local copies, waits for them, and re-layouts: 3.16 us -> 0.75 us
    convert_element_type x0 -> x1, other arithmetic: none -> 2.23 us  [shards(): return (jnp.transpose(grad_weight, (1, 0, 2)).astype(F32), grad_input)]
where the time goes in v4:
time: 95.4 us; the launch traced here: 94.5 us
  Pallas kernels  90.9 us (95%)
  other arithmetic  2.23 us (2%)
    pallas_call x1, Pallas kernels, shards(): pl.pallas_call(kernel, out_shape=(jax.ShapeDtypeStruct((3, COLS, WIDTH),...  90.9 us
    convert_element_type x1, other arithmetic, shards(): return (jnp.transpose(grad_weight, (1, 0, 2)).astype(F32), grad_input)  2.23 us

profile of v4, /device:TPU:1, one launch (start us, length us, event | category | flops | bytes accessed | tf_op | source)
XLA Modules:
  0.0 94.5 jit_solution(6561904263048479335)
XLA Ops:
  0.6 90.9 %parallel_block_backward.1 = (bf16[3,384,256]{2,1,0:T(8,128)(2,1)}, bf16[512,384]{1,0:T(8,128)(2,1)}) custom-call(bf16[512,384]{1,0:T(8,128)(2,1)} %tok.1, f32[16,1,384]{2,1,0:T(1,128)} %bitcast.7, bf16[3,512,256]{2,1,0:T(8,128)(2,1)} %bitcast.6, bf16[512,256]{1,0:T(8,128)(2,1)} %og.1, bf16[3,6144,256]{2,1,0:T(8,128)(2,1)} %bitcast.5), custom_call_target="tpu_custom_call" | custom-call | flops 11000000512 | bytes 14000000 | tf_op jit(solution)/shard_map/parallel_block_backward/pallas_call | solution.py:574
  91.5 0.0 copy-start
  91.5 2.2 %convert_bitcast_fusion = f32[384,3,256]{2,0,1:T(8,128)} fusion(bf16[3,384,256]{2,1,0:T(8,128)(2,1)} %get-tuple-element.4), kind=kLoop, calls=%fused_computation | loop fusion | flops 294912 | bytes 1769472 | tf_op jit(solution)/shard_map/convert_element_type | solution.py:634
  93.7 0.0 copy-done
  93.7 0.7 copy.8
Async XLA Ops:
  91.5 2.2 %copy-start = (bf16[512,384]{1,0:T(8,128)(2,1)S(1)}, bf16[512,384]{1,0:T(8,128)(2,1)}, u32[]{:S(2)}) copy-start(bf16[512,384]{1,0:T(8,128)(2,1)} %get-tuple-element.9) | copy-start | bytes 1179652

commit v5 on v4

--- a/solution.py
+++ b/solution.py
@@ -497,6 +497,14 @@
     x_copy(0).wait_recv()
     core_add(0, 0, 0, [xland.at[0]])
 
+    y_full(0, 1, 0).wait_recv()
+    y_full(0, -1, 0).wait_recv()
+    finish(0, [yland.at[0], yland.at[1]])
+
+    @pl.when(c != x)
+    def _():
+        copy_a.start()
+
     for k in (6, 7):
         reduce(1, k).wait_recv()
         reduce(-1, k).wait_recv()
@@ -520,10 +528,6 @@
 
     lax.fori_loop(0, HALF // 64, in_step, 0)
 
-    y_full(0, 1, 0).wait_recv()
-    y_full(0, -1, 0).wait_recv()
-    finish(0, [yland.at[0], yland.at[1]])
-
     @pl.when(c == x)
     def _():
         fin[c] = last[0]
@@ -531,7 +535,6 @@
 
     @pl.when(c != x)
     def _():
-        copy_a.start()
         for h in range(2):
             remote(last.at[1], fin.at[h], f_s.at[1], f_r.at[h], at_x).wait_recv()
         copy_a.wait_send()

time: 95.4 us -> 95.4 us (level)
  no operation moved by 1% of the time
where the time goes in v5:
time: 95.4 us; the launch traced here: 94.5 us
  Pallas kernels  90.9 us (95%)
  other arithmetic  2.23 us (2%)
    pallas_call x1, Pallas kernels, shards(): pl.pallas_call(kernel, out_shape=(jax.ShapeDtypeStruct((3, COLS, WIDTH),...  90.9 us
    convert_element_type x1, other arithmetic, shards(): return (jnp.transpose(grad_weight, (1, 0, 2)).astype(F32), grad_input)  2.23 us

profile of v5, /device:TPU:1, one launch (start us, length us, event | category | flops | bytes accessed | tf_op | source)
XLA Modules:
  0.0 94.5 jit_solution(2640201388622671779)
XLA Ops:
  0.6 90.9 %parallel_block_backward.1 = (bf16[3,384,256]{2,1,0:T(8,128)(2,1)}, bf16[512,384]{1,0:T(8,128)(2,1)}) custom-call(bf16[512,384]{1,0:T(8,128)(2,1)} %tok.1, f32[16,1,384]{2,1,0:T(1,128)} %bitcast.7, bf16[3,512,256]{2,1,0:T(8,128)(2,1)} %bitcast.6, bf16[512,256]{1,0:T(8,128)(2,1)} %og.1, bf16[3,6144,256]{2,1,0:T(8,128)(2,1)} %bitcast.5), custom_call_target="tpu_custom_call" | custom-call | flops 11000000512 | bytes 14000000 | tf_op jit(solution)/shard_map/parallel_block_backward/pallas_call | solution.py:577
  91.5 0.0 copy-start
  91.5 2.2 %convert_bitcast_fusion = f32[384,3,256]{2,0,1:T(8,128)} fusion(bf16[3,384,256]{2,1,0:T(8,128)(2,1)} %get-tuple-element.4), kind=kLoop, calls=%fused_computation | loop fusion | flops 294912 | bytes 1769472 | tf_op jit(solution)/shard_map/convert_element_type | solution.py:637
  93.7 0.0 copy-done
  93.7 0.7 copy.8
Async XLA Ops:
  91.5 2.2 %copy-start = (bf16[512,384]{1,0:T(8,128)(2,1)S(1)}, bf16[512,384]{1,0:T(8,128)(2,1)}, u32[]{:S(2)}) copy-start(bf16[512,384]{1,0:T(8,128)(2,1)} %get-tuple-element.9) | copy-start | bytes 1179652
